TPU v7x, 256 devices: a whole 4x4x8 slice. The times are simulated.
256 devices in a mesh: rep: 32 (over z, x_lo, core), shard: 8 (over y, x_hi).
Axes of the slice: x: 4 (x_hi: 2, x_lo: 2; x = x_hi * 2 + x_lo), y: 4, z: 8, core: 2. Of those that a mesh axis runs over, the one named last changes fastest.
Arguments:
- tokens: bfloat16 [32, 2048, 5120], P('rep', 'shard'), may hold values from -6 to 6
- cotangent: bfloat16 [32, 2048, 1024], P('rep', 'shard'), may hold values from -6 to 6
- weight: bfloat16 [5120, 1024], P('shard'), may hold values from -0.078125 to 0.078125
- momentum: float32 [32, 5120, 1024], P('rep', 'shard'), may hold values from -6 to 6
- gain: float32 [1024], replicated, may hold values from 0.1 to 1.9
- band: int32 [640], replicated, may hold values from 0 to 2015, as said below
Outputs:
- input_grad: bfloat16 [32, 2048, 5120], P('rep', 'shard')
- residue: float32 [32, 5120, 1024], P('rep', 'shard')
- update: bfloat16 [5120, 1024], P('shard')
Inputs may be any that keep to these rules, and one draw needn't show every extreme that they name: `band`: 640 distinct positions u * 64 + v with u and v both below 32, used for every block.
All inputs are finite; a program needn't handle non-finite values.
Results may differ from a plain program's by a relative error of at most 0.015.
Values may be sent and summed in bfloat16 or wider, within the bound.
No kernel may reach another device: no remote copies, remote signals or barrier semaphores. Data moves between devices by JAX's collectives and lax.ppermute only.
A program may use at most 128 MiB of HBM per device.

v0:
```python
import math
import jax
import jax.numpy as jnp
from jax import lax
from jax.sharding import PartitionSpec as P

norm_epsilon = 1e-06
block_epsilon = 1e-06
decay_rate = 0.999
step_rate = 0.02


def cosine_table():
    freq = jnp.arange(64, dtype=jnp.float32)
    angle = math.pi * (2.0 * freq[None, :] + 1.0) * freq[:, None] / 128.0
    factor = jnp.where(freq[:, None] == 0.0, math.sqrt(1.0 / 64.0), math.sqrt(2.0 / 64.0))
    return (factor * jnp.cos(angle))[:32]


def corner_index(band):
    return band // 64 * 32 + band % 64


def spread_table(corner):
    return (corner[None, :] == jnp.arange(1024, dtype=jnp.int32)[:, None]).astype(jnp.float32)


def forward_coeffs(matrix, table):
    row_count, col_count = matrix.shape
    blocks = matrix.reshape(row_count // 64, 64, col_count // 64, 64)
    coeffs = jnp.einsum("ua,iajb,vb->ijuv", table, blocks, table, precision=lax.Precision.HIGHEST)
    return coeffs.reshape(-1, 1024)


def inverse_coeffs(coeffs, table, row_count, col_count):
    square = coeffs.reshape(row_count // 64, col_count // 64, 32, 32)
    blocks = jnp.einsum("ua,ijuv,vb->iajb", table, square, table, precision=lax.Precision.HIGHEST)
    return blocks.reshape(row_count, col_count)


def band_spread(picked, spread):
    return lax.dot_general(
        picked, spread, (((1,), (1,)), ((), ())), precision=lax.Precision.HIGHEST
    )


def block_normalize(matrix):
    row_count, col_count = matrix.shape
    blocks = matrix.reshape(row_count // 64, 64, col_count // 64, 64)
    mean_square = jnp.mean(blocks * blocks, axis=(1, 3), keepdims=True)
    return (blocks * lax.rsqrt(mean_square + block_epsilon)).reshape(row_count, col_count)


def key_gradient(projected, upstream, gain):
    mean_square = jnp.mean(projected * projected, axis=-1, keepdims=True)
    inverse = lax.rsqrt(mean_square + norm_epsilon)
    scaled = upstream.astype(jnp.float32) * gain[None, :]
    projection = jnp.mean(scaled * projected, axis=-1, keepdims=True)
    key_grad = inverse * (scaled - projected * inverse * inverse * projection)
    return key_grad.astype(jnp.bfloat16)


def per_device(tokens, cotangent, weight, momentum, gain, band):
    activations = tokens[0]
    upstream = cotangent[0]
    local_rows = weight.shape[0]
    features = weight.shape[1]
    table = cosine_table()
    corner = corner_index(band)
    spread = spread_table(corner)
    gathered = lax.all_gather(weight, "shard", axis=0, tiled=True)
    projected = jnp.dot(activations, gathered, preferred_element_type=jnp.float32)
    key_grad = key_gradient(projected, upstream, gain)
    input_grad = lax.dot_general(
        key_grad, gathered, (((1,), (1,)), ((), ())), preferred_element_type=jnp.float32
    )
    input_grad = input_grad.astype(jnp.bfloat16)
    gradient = lax.psum_scatter(
        lax.dot_general(
            activations, key_grad, (((0,), (0,)), ((), ())), preferred_element_type=jnp.float32
        ).astype(jnp.bfloat16),
        "shard",
        scatter_dimension=0,
        tiled=True,
    ).astype(jnp.float32)
    blended = decay_rate * momentum[0] + step_rate * gradient
    coeffs = forward_coeffs(blended, table)
    picked = jnp.take(coeffs, corner, axis=1)
    residue = blended - inverse_coeffs(band_spread(picked, spread), table, local_rows, features)
    all_bands = lax.all_gather(picked[None].astype(jnp.bfloat16), "rep", axis=0, tiled=True).astype(
        jnp.float32
    )
    summed = jnp.sum(all_bands, axis=0)
    combined = inverse_coeffs(band_spread(summed, spread), table, local_rows, features)
    update = block_normalize(combined).astype(jnp.bfloat16)
    return (input_grad[None], residue[None], update)


def solution(mesh):
    return jax.shard_map(
        per_device,
        mesh=mesh,
        in_specs=(
            P("rep", "shard", None),
            P("rep", "shard", None),
            P("shard", None),
            P("rep", "shard", None),
            P(),
            P(),
        ),
        out_specs=(P("rep", "shard", None), P("rep", "shard", None), P("shard", None)),
        check_vma=False,
    )
```

profile of v0, /device:TPU:1, one launch (start us, length us, event | category | flops | bytes accessed | tf_op | source)
XLA Modules:
  0.0 442.0 jit_solution(4065398100505784047)
XLA Ops:
  7.2 0.0 copy-start
  7.2 0.0 all-gather.3.cloned.1.call-start
  7.2 0.7 all-gather.3.cloned.1.call-update
  7.9 0.0 copy-start.4
  7.9 0.0 copy-start.5
  7.9 0.0 reduce-scatter.4.cloned.1.call-start
  8.0 137.1 %all-gather.3.cloned.1.call-done = bf16[5120,1024]{1,0:T(8,128)(2,1)} async-done(((bf16[640,1024]{1,0:T(8,128)(2,1)}), bf16[5120,1024]{1,0:T(8,128)(2,1)}) %all-gather.3.cloned.1.call-update) | async-done | bytes 10485776 | tf_op jit(solution)/shard_map/all_gather | solution.py:71
  145.1 0.0 copy-done
  145.1 7.1 %multiply_reduce_fusion.1 = (f32[256]{0:T(256)S(1)}, f32[256]{0:T(256)S(1)}, f32[256,1024]{1,0:T(8,128)S(1)}) fusion(f32[1024]{0:T(1024)} %param.10, bf16[1,256,1024]{2,1,0:T(8,128)(2,1)} %param.7, bf16[5120,1024]{1,0:T(8,128)(2,1)} %all-gather.3.cloned.1.call-done, bf16[1,256,5120]{2,1,0:T(8,128)(2,1)S(1)} %copy-done), kind=kOutput, calls=%fused_computation.32 | convolution fusion | flops 2685926912 | bytes 14686208 | tf_op jit(solution)/shard_map/dot_general | solution.py:72
  152.2 0.0 copy-start.3
  152.2 1.0 copy-done.3
  153.1 0.0 copy-done.4
  153.1 0.0 copy-done.5
  153.1 5.8 %convert_bitcast_fusion = bf16[5120,1024]{0,1:T(8,128)(2,1)} fusion(bf16[1,256,5120]{2,1,0:T(8,128)(2,1)S(1)} %copy-done, f32[256,1024]{1,0:T(8,128)S(1)} %get-tuple-element.13, bf16[1,256,1024]{2,1,0:T(8,128)(2,1)S(1)} %copy-done.4, f32[256]{0:T(256)S(1)} %get-tuple-element.17, f32[1024]{0:T(1024)S(1)} %copy-done.5, f32[256]{0:T(256)S(1)} %get-tuple-element.16), kind=kOutput, calls=%fused_computation.2 | convolution fusion | flops 2691694592 | bytes 14686208 | tf_op jit(solution)/shard_map/dot_general | solution.py:79
  158.9 14.4 %copy.53 = bf16[5120,1024]{1,0:T(8,128)(2,1)} copy(bf16[5120,1024]{0,1:T(8,128)(2,1)} %convert_bitcast_fusion) | data formatting | bytes 20971520
  173.3 0.0 copy-start.6
  173.3 0.0 reduce-scatter.4.cloned.1.call-update
  173.4 0.6 all-gather.5.cloned.1.call-start
  174.0 0.1 copy-done.6
  174.1 135.4 %reduce-scatter.4.cloned.1.call-done = bf16[640,1024]{1,0:T(8,128)(2,1)} async-done(((bf16[5120,1024]{1,0:T(8,128)(2,1)}), bf16[640,1024]{1,0:T(8,128)(2,1)}) %reduce-scatter.4.cloned.1.call-update) | async-done | bytes 1310736 | tf_op jit(solution)/shard_map/reduce_scatter | solution.py:78
  309.5 2.8 bitcast_add_fusion
  312.3 3.1 reshape.117
  315.4 6.9 %fusion.1 = f32[10,16,64,32]{2,3,1,0:T(8,128)S(1)} fusion(f32[10,64,16,64]{3,2,1,0:T(8,128)} %reshape.117, f32[32]{0:T(128)S(1)} %bitcast.69, f32[64]{0:T(128)S(1)} %add_multiply_fusion.1), kind=kOutput, calls=%fused_computation.5 | convolution fusion | flops 251668480 | bytes 3932544 | tf_op jit(solution)/shard_map/ua,iajb,vb->ijuv/dot_general | solution.py:31
  322.3 3.7 fusion.34
  326.1 2.7 reshape.118
  328.8 1.3 copy.42
  330.1 3.6 gather_fusion
  333.7 1.0 copy.43
  334.6 1.7 fusion.21
  336.3 0.0 all-gather.5.cloned.1.call-update
  336.4 0.0 copy-start.2
  336.4 9.0 %fusion = bf16[1,256,5120]{2,1,0:T(8,128)(2,1)} fusion(bf16[5120,1024]{1,0:T(8,128)(2,1)} %all-gather.3.cloned.1.call-done, f32[256,1024]{1,0:T(8,128)} %copy-done.3, bf16[1,256,1024]{2,1,0:T(8,128)(2,1)} %param.7, f32[256]{0:T(256)S(1)} %get-tuple-element.17, f32[1024]{0:T(1024)S(1)} %copy-done.5, f32[256]{0:T(256)S(1)} %get-tuple-element.16), kind=kOutput, calls=%fused_computation.4 | convolution fusion | flops 2687762432 | bytes 14686208 | tf_op jit(solution)/shard_map/dot_general | solution.py:74
  345.4 0.0 copy-done.2
  345.4 1.6 fusion.9
  347.0 2.4 reshape.119
  349.4 6.2 %fusion.32 = f32[10,16,32,64]{3,2,1,0:T(8,128)S(1)} fusion(f32[10,16,32,32]{3,2,1,0:T(8,128)} %reshape.119, f32[32]{0:T(128)S(1)} %bitcast.71, f32[64]{0:T(128)S(1)} %add_multiply_fusion.1), kind=kOutput, calls=%fused_computation.44 | convolution fusion | flops 125839360 | bytes 1966464 | tf_op jit(solution)/shard_map/ua,ijuv,vb->iajb/dot_general | solution.py:37
  355.6 8.6 %convolution_bitcast_fusion = f32[10,64,16,64]{3,1,2,0:T(8,128)S(1)} fusion(f32[10,16,32,64]{3,2,1,0:T(8,128)S(1)} %fusion.32, f32[32]{0:T(128)S(1)} %bitcast.72, f32[64]{0:T(128)S(1)} %add_multiply_fusion.1), kind=kOutput, calls=%fused_computation.22 | convolution fusion | flops 251668480 | bytes 3932544 | tf_op jit(solution)/shard_map/ua,ijuv,vb->iajb/dot_general | solution.py:37
  364.1 5.5 %copy.45 = f32[10,64,16,64]{3,2,1,0:T(8,128)} copy(f32[10,64,16,64]{3,1,2,0:T(8,128)S(1)} %convolution_bitcast_fusion) | data formatting | bytes 5242880 | tf_op jit(solution)/shard_map/ua,ijuv,vb->iajb/transpose | solution.py:37
  369.7 5.6 %reshape.120 = f32[640,1024]{1,0:T(8,128)} reshape(f32[10,64,16,64]{3,2,1,0:T(8,128)} %copy.45) | data formatting | bytes 5242880 | tf_op jit(solution)/shard_map/reshape | solution.py:38
  375.3 4.0 subtract_bitcast_fusion
  379.3 26.7 %all-gather.5.cloned.1.call-done = bf16[32,160,640]{2,1,0:T(8,128)(2,1)} async-done(((bf16[1,160,640]{2,1,0:T(8,128)(2,1)}), bf16[32,160,640]{2,1,0:T(8,128)(2,1)}) %all-gather.5.cloned.1.call-update) | async-done | bytes 6553616 | tf_op jit(solution)/shard_map/all_gather | solution.py:90
  406.0 4.0 convert_reduce_fusion
  410.0 3.3 fusion.10
  413.3 4.6 %fusion.7 = f32[10,16,32,64]{3,2,1,0:T(8,128)S(1)} fusion(f32[10,16,32,32]{3,1,2,0:T(8,128)S(1)} %fusion.10, f32[32]{0:T(128)S(1)} %bitcast.73, f32[64]{0:T(128)S(1)} %add_multiply_fusion.1), kind=kOutput, calls=%fused_computation.14 | convolution fusion | flops 125839360 | bytes 1966464 | tf_op jit(solution)/shard_map/ua,ijuv,vb->iajb/dot_general | solution.py:37
  417.9 8.9 %multiply_reduce_fusion = (f32[10,16]{1,0:T(8,128)S(1)}, f32[10,16,64,64]{3,2,1,0:T(8,128)S(1)}) fusion(f32[10,16,32,64]{3,2,1,0:T(8,128)S(1)} %fusion.7, f32[32]{0:T(128)S(1)} %bitcast.74, f32[64]{0:T(128)S(1)} %add_multiply_fusion.1), kind=kOutput, calls=%fused_computation.8 | convolution fusion | flops 252979040 | bytes 3933184 | tf_op jit(solution)/shard_map/ua,ijuv,vb->iajb/dot_general | solution.py:37
  426.8 0.5 fusion.3
  427.3 0.0 copy-start.1
  427.3 3.5 copy.49
  430.8 4.5 %convert_element_type.56 = bf16[640,1024]{1,0:T(8,128)(2,1)} reshape(bf16[10,64,16,64]{3,2,1,0:T(8,128)(2,1)} %copy.49) | data formatting | bytes 2621440 | tf_op jit(solution)/shard_map/convert_element_type | solution.py:95
  435.3 0.0 copy-done.1
  (8 shorter events, 0.1 us)
Async XLA Ops:
  7.2 137.9 %copy-start = (bf16[1,256,5120]{2,1,0:T(8,128)(2,1)S(1)}, bf16[1,256,5120]{2,1,0:T(8,128)(2,1)}, u32[]{:S(2)}) copy-start(bf16[1,256,5120]{2,1,0:T(8,128)(2,1)} %param.6) | copy-start | bytes 7864324
  7.2 137.9 %all-gather.3.cloned.1.call-start = ((), (), s32[]{:S(2)}) async-start(), calls=%async_computation.1 | async-start | bytes 11796480 | tf_op jit(solution)/shard_map/all_gather | solution.py:71
  7.9 145.2 %copy-start.4 = (bf16[1,256,1024]{2,1,0:T(8,128)(2,1)S(1)}, bf16[1,256,1024]{2,1,0:T(8,128)(2,1)}, u32[]{:S(2)}) copy-start(bf16[1,256,1024]{2,1,0:T(8,128)(2,1)} %param.7) | copy-start | bytes 1572868
  7.9 145.2 %copy-start.5 = (f32[1024]{0:T(1024)S(1)}, f32[1024]{0:T(1024)}, u32[]{:S(2)}) copy-start(f32[1024]{0:T(1024)} %param.10) | copy-start | bytes 12292
  7.9 301.6 %reduce-scatter.4.cloned.1.call-start = ((), (), s32[]{:S(2)}) async-start(), calls=%async_computation.3 | async-start | bytes 11796480 | tf_op jit(solution)/shard_map/reduce_scatter | solution.py:78
  152.2 1.0 copy-start.3
  173.3 0.7 copy-start.6
  173.4 232.7 %all-gather.5.cloned.1.call-start = ((), (), s32[]{:S(2)}) async-start(), calls=%async_computation.2 | async-start | bytes 6758400 | tf_op jit(solution)/shard_map/all_gather | solution.py:90
  336.4 9.0 %copy-start.2 = (f32[640,160]{0,1:T(8,128)S(1)}, f32[640,160]{0,1:T(8,128)}, u32[]{:S(2)}) copy-start(f32[640,160]{0,1:T(8,128)} %copy.43) | copy-start | bytes 1228804
  427.3 8.0 %copy-start.1 = (bf16[1,256,5120]{2,1,0:T(8,128)(2,1)S(1)}, bf16[1,256,5120]{2,1,0:T(8,128)(2,1)}, u32[]{:S(2)}) copy-start(bf16[1,256,5120]{2,1,0:T(8,128)(2,1)} %param.6) | copy-start | bytes 7864324
Sparse Core Ops, SparseCore 0:
  10.6 134.4 all-gather.2
  173.5 135.9 reduce-scatter.3
  336.5 69.4 all-gather.4
where the time goes:
time: 447 us; the launch traced here: 442 us
  waiting for transfers between devices  300 us (67%)
  matrix products  65.7 us (15%)
  local copies, waits for them, and re-layouts  48.5 us (11%)
  between operations  14.1 us (3%)
  other arithmetic  13.1 us (3%)
    all_gather x1, waiting for transfers between devices, per_device(): gathered = lax.all_gather(weight, 'shard', axis=0, tiled=True)  137 us
    reduce_scatter x1, waiting for transfers between devices, per_device(): lax.psum_scatter(lax.dot_general(activations, key_grad, (((0,), (0,)), ((...  135 us
    dot_general x4, matrix products, inverse_coeffs(): jnp.einsum('ua,ijuv,vb->iajb', table, square, table, precision=lax.Precis...  28.2 us
    all_gather x1, waiting for transfers between devices, per_device(): lax.all_gather(picked[None].astype(jnp.bfloat16), 'rep', axis=0, tiled=True)  26.7 us
    unnamed x15, local copies, waits for them, and re-layouts  15.4 us
    dot_general x2, matrix products, forward_coeffs(): jnp.einsum('ua,iajb,vb->ijuv', table, blocks, table, precision=lax.Precis...  10.7 us
    dot_general x1, matrix products, per_device(): lax.dot_general(key_grad, gathered, (((1,), (1,)), ((), ())), preferred_e...  9.01 us
  transfers between devices with their start and end apart: 3, of which 3 were waited for; matrix products, arithmetic and copies ran while one was open for 10% of the time, Pallas kernels for 0%

commit v1 on v0

--- a/solution.py
+++ b/solution.py
@@ -87,9 +87,12 @@
     coeffs = forward_coeffs(blended, table)
     picked = jnp.take(coeffs, corner, axis=1)
     residue = blended - inverse_coeffs(band_spread(picked, spread), table, local_rows, features)
-    all_bands = lax.all_gather(picked[None].astype(jnp.bfloat16), "rep", axis=0, tiled=True).astype(
-        jnp.float32
-    )
+    all_bands = jnp.concatenate(
+        lax.all_to_all(
+            jnp.stack([picked[None].astype(jnp.bfloat16)] * lax.axis_size("rep")), "rep", 0, 0
+        ),
+        axis=0,
+    ).astype(jnp.float32)
     summed = jnp.sum(all_bands, axis=0)
     combined = inverse_coeffs(band_spread(summed, spread), table, local_rows, features)
     update = block_normalize(combined).astype(jnp.bfloat16)

time: 447 us -> 536 us (1.20)
  waiting for transfers between devices: 300 us -> 376 us
  starting transfers between devices: 0.64 us -> 9.13 us
    all_to_all x0 -> x1, waiting for transfers between devices: none -> 102 us  [per_device(): lax.all_to_all(jnp.stack([picked[None].astype(jnp.bfloat16)] * lax.axis_s...]
    all_gather x1 -> x0, waiting for transfers between devices: 26.7 us -> none  [per_device(): lax.all_gather(picked[None].astype(jnp.bfloat16), 'rep', axis=0, tiled=True)]
    all_to_all x0 -> x1, starting transfers between devices: none -> 9.05 us  [per_device(): lax.all_to_all(jnp.stack([picked[None].astype(jnp.bfloat16)] * lax.axis_s...]
    unnamed x15 -> x13, local copies, waits for them, and re-layouts: 15.4 us -> 16 us
  transfers between devices with their start and end apart: 3 -> 3, of which waited for: 3 -> 3; matrix products, arithmetic and copies ran while one was open for 10% -> 8% of each run, Pallas kernels for 0% -> 0%
where the time goes in v1:
time: 536 us; the launch traced here: 532 us
  waiting for transfers between devices  376 us (70%)
  matrix products  67.5 us (13%)
  local copies, waits for them, and re-layouts  52.6 us (10%)
  between operations  14.4 us (3%)
  other arithmetic  12.2 us (2%)
  starting transfers between devices  9.13 us (2%)
    all_gather x1, waiting for transfers between devices, per_device(): gathered = lax.all_gather(weight, 'shard', axis=0, tiled=True)  137 us
    reduce_scatter x1, waiting for transfers between devices, per_device(): lax.psum_scatter(lax.dot_general(activations, key_grad, (((0,), (0,)), ((...  136 us
    all_to_all x1, waiting for transfers between devices, per_device(): lax.all_to_all(jnp.stack([picked[None].astype(jnp.bfloat16)] * lax.axis_s...  102 us
    dot_general x4, matrix products, inverse_coeffs(): jnp.einsum('ua,ijuv,vb->iajb', table, square, table, precision=lax.Precis...  28.2 us
    unnamed x13, local copies, waits for them, and re-layouts  16 us
  transfers between devices with their start and end apart: 3, of which 3 were waited for; matrix products, arithmetic and copies ran while one was open for 8% of the time, Pallas kernels for 0%

profile of v1, /device:TPU:1, one launch (start us, length us, event | category | flops | bytes accessed | tf_op | source)
XLA Modules:
  0.0 532.1 jit_solution(14170729261378974506)
XLA Ops:
  7.2 0.0 copy-start
  7.2 0.0 all-gather.2.cloned.1.call-start
  7.2 0.7 all-gather.2.cloned.1.call-update
  7.9 0.0 copy-start.3
  7.9 0.0 copy-start.4
  7.9 0.0 reduce-scatter.4.cloned.1.call-start
  8.0 137.1 %all-gather.2.cloned.1.call-done = bf16[5120,1024]{1,0:T(8,128)(2,1)} async-done(((bf16[640,1024]{1,0:T(8,128)(2,1)}), bf16[5120,1024]{1,0:T(8,128)(2,1)}) %all-gather.2.cloned.1.call-update) | async-done | bytes 10485776 | tf_op jit(solution)/shard_map/all_gather | solution.py:71
  145.1 0.0 copy-done
  145.1 7.1 %multiply_reduce_fusion.1 = (f32[256]{0:T(256)S(1)}, f32[256]{0:T(256)S(1)}, f32[256,1024]{1,0:T(8,128)S(1)}) fusion(f32[1024]{0:T(1024)} %param.10, bf16[1,256,1024]{2,1,0:T(8,128)(2,1)} %param.7, bf16[5120,1024]{1,0:T(8,128)(2,1)} %all-gather.2.cloned.1.call-done, bf16[1,256,5120]{2,1,0:T(8,128)(2,1)S(1)} %copy-done), kind=kOutput, calls=%fused_computation.32 | convolution fusion | flops 2685926912 | bytes 14686208 | tf_op jit(solution)/shard_map/dot_general | solution.py:72
  152.2 0.0 copy-start.2
  152.2 1.0 copy-done.2
  153.1 0.0 copy-done.3
  153.1 0.0 copy-done.4
  153.1 6.1 %convert_bitcast_fusion = bf16[5120,1024]{0,1:T(8,128)(2,1)} fusion(bf16[1,256,5120]{2,1,0:T(8,128)(2,1)S(1)} %copy-done, f32[256,1024]{1,0:T(8,128)S(1)} %get-tuple-element.13, bf16[1,256,1024]{2,1,0:T(8,128)(2,1)S(1)} %copy-done.3, f32[256]{0:T(256)S(1)} %get-tuple-element.17, f32[1024]{0:T(1024)S(1)} %copy-done.4, f32[256]{0:T(256)S(1)} %get-tuple-element.16), kind=kOutput, calls=%fused_computation.2 | convolution fusion | flops 2691694592 | bytes 14686208 | tf_op jit(solution)/shard_map/dot_general | solution.py:79
  159.2 14.4 %copy.41 = bf16[5120,1024]{1,0:T(8,128)(2,1)} copy(bf16[5120,1024]{0,1:T(8,128)(2,1)} %convert_bitcast_fusion) | data formatting | bytes 20971520
  173.6 0.0 copy-start.5
  173.6 0.0 reduce-scatter.4.cloned.1.call-update
  173.7 0.6 copy-done.5
  174.3 135.9 %reduce-scatter.4.cloned.1.call-done = bf16[640,1024]{1,0:T(8,128)(2,1)} async-done(((bf16[5120,1024]{1,0:T(8,128)(2,1)}), bf16[640,1024]{1,0:T(8,128)(2,1)}) %reduce-scatter.4.cloned.1.call-update) | async-done | bytes 1310736 | tf_op jit(solution)/shard_map/reduce_scatter | solution.py:78
  310.2 2.8 bitcast_add_fusion
  313.0 3.1 reshape.115
  316.1 6.9 %fusion.1 = f32[10,16,64,32]{2,3,1,0:T(8,128)S(1)} fusion(f32[10,64,16,64]{3,2,1,0:T(8,128)} %reshape.115, f32[32]{0:T(128)S(1)} %bitcast.63, f32[64]{0:T(128)S(1)} %add_multiply_fusion.1), kind=kOutput, calls=%fused_computation.5 | convolution fusion | flops 251668480 | bytes 3932544 | tf_op jit(solution)/shard_map/ua,iajb,vb->ijuv/dot_general | solution.py:31
  323.1 3.8 fusion.35
  326.8 2.7 reshape.116
  329.5 1.3 copy.32
  330.8 3.4 gather_fusion
  334.3 0.9 fusion.22
  335.1 1.1 copy.35
  336.3 3.2 stack.2
  339.5 9.1 %all-to-all-start = ((bf16[32,1,160,640]{3,2,1,0:T(8,128)(2,1)}), bf16[32,1,160,640]{3,2,1,0:T(8,128)(2,1)}, u32[]{:S(2)}, u32[]{:S(2)}) async-start(bf16[32,1,160,640]{3,2,1,0:T(8,128)(2,1)} %stack.2), calls=%async_computation | async-start | bytes 13107200 | tf_op jit(solution)/shard_map/all_to_all | solution.py:91
  348.6 9.0 %fusion = bf16[1,256,5120]{2,1,0:T(8,128)(2,1)} fusion(bf16[5120,1024]{1,0:T(8,128)(2,1)} %all-gather.2.cloned.1.call-done, f32[256,1024]{1,0:T(8,128)} %copy-done.2, bf16[1,256,1024]{2,1,0:T(8,128)(2,1)} %param.7, f32[256]{0:T(256)S(1)} %get-tuple-element.17, f32[1024]{0:T(1024)S(1)} %copy-done.4, f32[256]{0:T(256)S(1)} %get-tuple-element.16), kind=kOutput, calls=%fused_computation.4 | convolution fusion | flops 2687762432 | bytes 14686208 | tf_op jit(solution)/shard_map/dot_general | solution.py:74
  357.5 3.2 fusion.9
  360.8 3.1 reshape.117
  363.8 6.1 %fusion.33 = f32[10,16,32,64]{3,2,1,0:T(8,128)S(1)} fusion(f32[10,16,32,32]{3,2,1,0:T(8,128)} %reshape.117, f32[32]{0:T(128)S(1)} %bitcast.65, f32[64]{0:T(128)S(1)} %add_multiply_fusion.1), kind=kOutput, calls=%fused_computation.44 | convolution fusion | flops 125839360 | bytes 1966464 | tf_op jit(solution)/shard_map/ua,ijuv,vb->iajb/dot_general | solution.py:37
  370.0 8.5 %convolution_bitcast_fusion = f32[10,64,16,64]{3,1,2,0:T(8,128)S(1)} fusion(f32[10,16,32,64]{3,2,1,0:T(8,128)S(1)} %fusion.33, f32[32]{0:T(128)S(1)} %bitcast.66, f32[64]{0:T(128)S(1)} %add_multiply_fusion.1), kind=kOutput, calls=%fused_computation.22 | convolution fusion | flops 251668480 | bytes 3932544 | tf_op jit(solution)/shard_map/ua,ijuv,vb->iajb/dot_general | solution.py:37
  378.5 5.5 %copy.34 = f32[10,64,16,64]{3,2,1,0:T(8,128)} copy(f32[10,64,16,64]{3,1,2,0:T(8,128)S(1)} %convolution_bitcast_fusion) | data formatting | bytes 5242880 | tf_op jit(solution)/shard_map/ua,ijuv,vb->iajb/transpose | solution.py:37
  384.0 5.2 reshape.118
  389.2 4.0 subtract_bitcast_fusion
  393.2 102.5 %all-to-all-done = bf16[32,1,160,640]{3,2,1,0:T(8,128)(2,1)} async-done(((bf16[32,1,160,640]{3,2,1,0:T(8,128)(2,1)}), bf16[32,1,160,640]{3,2,1,0:T(8,128)(2,1)}, u32[]{:S(2)}, u32[]{:S(2)}) %all-to-all-start) | async-done | bytes 6553632 | tf_op jit(solution)/shard_map/all_to_all | solution.py:91
  495.7 4.0 convert_reduce_fusion
  499.6 3.3 fusion.10
  503.0 4.6 fusion.7
  507.6 8.9 %multiply_reduce_fusion = (f32[10,16]{1,0:T(8,128)S(1)}, f32[10,16,64,64]{3,2,1,0:T(8,128)S(1)}) fusion(f32[10,16,32,64]{3,2,1,0:T(8,128)S(1)} %fusion.7, f32[32]{0:T(128)S(1)} %bitcast.68, f32[64]{0:T(128)S(1)} %add_multiply_fusion.1), kind=kOutput, calls=%fused_computation.8 | convolution fusion | flops 252979040 | bytes 3933184 | tf_op jit(solution)/shard_map/ua,ijuv,vb->iajb/dot_general | solution.py:37
  516.5 0.5 fusion.3
  517.0 0.0 copy-start.1
  517.0 3.5 copy.37
  520.5 4.5 convert_element_type.56
  525.0 0.0 copy-done.1
  (8 shorter events, 0.1 us)
Async XLA Ops:
  7.2 137.9 %copy-start = (bf16[1,256,5120]{2,1,0:T(8,128)(2,1)S(1)}, bf16[1,256,5120]{2,1,0:T(8,128)(2,1)}, u32[]{:S(2)}) copy-start(bf16[1,256,5120]{2,1,0:T(8,128)(2,1)} %param.6) | copy-start | bytes 7864324
  7.2 137.9 %all-gather.2.cloned.1.call-start = ((), (), s32[]{:S(2)}) async-start(), calls=%async_computation.2 | async-start | bytes 11796480 | tf_op jit(solution)/shard_map/all_gather | solution.py:71
  7.9 145.2 %copy-start.3 = (bf16[1,256,1024]{2,1,0:T(8,128)(2,1)S(1)}, bf16[1,256,1024]{2,1,0:T(8,128)(2,1)}, u32[]{:S(2)}) copy-start(bf16[1,256,1024]{2,1,0:T(8,128)(2,1)} %param.7) | copy-start | bytes 1572868
  7.9 145.2 %copy-start.4 = (f32[1024]{0:T(1024)S(1)}, f32[1024]{0:T(1024)}, u32[]{:S(2)}) copy-start(f32[1024]{0:T(1024)} %param.10) | copy-start | bytes 12292
  7.9 302.3 %reduce-scatter.4.cloned.1.call-start = ((), (), s32[]{:S(2)}) async-start(), calls=%async_computation.3 | async-start | bytes 11796480 | tf_op jit(solution)/shard_map/reduce_scatter | solution.py:78
  152.2 1.0 copy-start.2
  173.6 0.7 copy-start.5
  339.5 156.2 %all-to-all-start = ((bf16[32,1,160,640]{3,2,1,0:T(8,128)(2,1)}), bf16[32,1,160,640]{3,2,1,0:T(8,128)(2,1)}, u32[]{:S(2)}, u32[]{:S(2)}) async-start(bf16[32,1,160,640]{3,2,1,0:T(8,128)(2,1)} %stack.2), calls=%async_computation | async-start | bytes 13107200 | tf_op jit(solution)/shard_map/all_to_all | solution.py:91
  517.0 8.0 %copy-start.1 = (bf16[1,256,5120]{2,1,0:T(8,128)(2,1)S(1)}, bf16[1,256,5120]{2,1,0:T(8,128)(2,1)}, u32[]{:S(2)}) copy-start(bf16[1,256,5120]{2,1,0:T(8,128)(2,1)} %param.6) | copy-start | bytes 7864324
Sparse Core Ops, SparseCore 0:
  10.6 134.4 all-gather.1
  173.8 136.4 reduce-scatter.3
